TPU v7x, 256 devices: a whole 4x4x8 slice. The times are simulated.
256 devices in a mesh: dp: 4 (over x_hi, core), ctx: 64 (over z, x_lo, y).
Axes of the slice: x: 4 (x_hi: 2, x_lo: 2; x = x_hi * 2 + x_lo), y: 4, z: 8, core: 2. Of those that a mesh axis runs over, the one named last changes fastest.
Arguments:
- grad_output: bfloat16 [4, 2048, 8192], P('dp', None, 'ctx'), may hold values from -6 to 6
- post_gate: bfloat16 [4, 2048, 8192], P('dp', None, 'ctx'), may hold values from -6 to 6
- pre_gate: bfloat16 [4, 2048, 8192], P('dp', None, 'ctx'), may hold values from -6 to 6
- value_branch: bfloat16 [4, 2048, 8192], P('dp', None, 'ctx'), may hold values from -6 to 6
- long_filter: float32 [2048, 8192], P('ctx'), may hold values from -0.0625 to 0.0625
- skip_weight: float32 [2048], replicated, may hold values from -3 to 3
Outputs:
- grad_pre_gate: bfloat16 [4, 2048, 8192], P('dp', None, 'ctx')
- grad_value_branch: bfloat16 [4, 2048, 8192], P('dp', None, 'ctx')
- grad_long_filter: float32 [2048, 8192], P('ctx', 'dp')
All inputs are finite; a program needn't handle non-finite values.
Results may differ from a plain program's by a relative error of at most 0.0095.
Values may be sent and summed in bfloat16 or wider, within the bound.
A program may use at most 64 MiB of HBM per device.

v0:
```python
import functools
import math

import jax
import jax.numpy as jnp
from jax import lax
from jax.experimental import pallas as pl
from jax.experimental.pallas import tpu as pltpu
from jax.sharding import PartitionSpec as P


f32, bf16 = jnp.float32, jnp.bfloat16
B = 128
W = 2048


def row_bits(shape):
    return lax.broadcasted_iota(jnp.int32, shape, 0)


def stagger(v, left):
    width = v.shape[1]
    rows = row_bits(v.shape)
    for bit in (1, 2, 4):
        moved = pltpu.roll(v, (width - bit) if left else bit, 1)
        v = jnp.where((rows & bit) != 0, moved, v)
    return v


def build_filters(fpad, toep):
    length = toep.shape[2]

    @pl.loop(0, 8)
    def _(c):
        @pl.loop(0, length // W)
        def _(w):
            lanes = pl.ds(pl.multiple_of(w * W, W), W + B)
            v = jnp.broadcast_to(fpad[pl.ds(c, 1), lanes], (8, W + B))
            v = stagger(v, False)
            for a in range(0, 16, 2):
                lo = v if a == 0 else pltpu.roll(v, 8 * a, 1)
                hi = pltpu.roll(v, 8 * a + 8, 1)
                both = jnp.concatenate([lo[:, B:], hi[:, B:]], 0).astype(bf16)
                toep[c, pl.ds(8 * a, 16), pl.ds(pl.multiple_of(w * W, W), W)] = both


def shifted(rows, out, c):
    for p in range(4):
        out[c, p, pl.ds(0, 256), :] = rows[pl.ds(c + 32 * p, 256, stride=8), :].astype(bf16)


def correlate(toep, shifts, c):
    acc = jnp.zeros((256, B), f32)
    for d4 in range(16):
        live = 256 - 16 * d4
        part = jnp.zeros((live, B), f32)
        for h in range(2):
            lhs = jnp.concatenate([shifts[c, 2 * h + e, pl.ds(16 * d4, live), :] for e in range(2)], 1)
            rhs = toep[c, :, pl.ds((4 * d4 + 2 * h) * B, 2 * B)]
            part += lax.dot_general(lhs, rhs, (((1,), (1,)), ((), ())), preferred_element_type=f32)
        if live == 256:
            acc += part
        else:
            acc = jnp.concatenate([acc[:live] + part, acc[live:]], 0)
    return acc


PITCH = 136
HALF = 4

def product_blocks(saved_t, shifts, blocks, c, slot):
    for d4 in range(16):
        depth = 256 if d4 < 8 else 128
        for h in range(2):
            m = 4 * d4 + 2 * h
            rhs = jnp.concatenate([shifts[c, 2 * h + e, pl.ds(16 * d4, depth), :] for e in range(2)], 1)
            out = jnp.dot(saved_t[:, :depth], rhs, preferred_element_type=f32)
            for e in range(2):
                blocks[pl.ds(pl.multiple_of((slot * 64 + m + e) * PITCH, 8), B), :] = out[:, e * B:(e + 1) * B]

def fold(blocks, totals, step=8):
    totals[...] = jnp.zeros(totals.shape, f32)
    rows = totals.shape[0]
    k = lax.broadcasted_iota(jnp.int32, (B, 2 * B), 0)
    n = lax.broadcasted_iota(jnp.int32, (B, 2 * B), 1)
    gap = n - k - B

    @pl.loop(0, B // step)
    def _(t):
        lhs, rhs = [], []
        for e in range(step):
            jp = t * step + e
            lhs.append(blocks[pl.ds(jp, rows, stride=PITCH), :].astype(bf16))
            rhs.append(jnp.where(gap == -jp, 1.0, 0.0).astype(bf16))
        totals[...] += jnp.dot(jnp.concatenate(lhs, 1), jnp.concatenate(rhs, 0), preferred_element_type=f32)


def conv_kernel(f_ref, g_ref, s_ref, c_ref, d_ref, fpad, toep, grows, srows, shifts, crows, blocks, totals):
    length = toep.shape[2]
    fpad[:, :B] = jnp.zeros((8, B), f32)
    fpad[:, pl.ds(B, length)] = f_ref[...]
    build_filters(fpad, toep)
    for z in range(8):
        grows[pl.ds(z * 256, 256), :] = g_ref[pl.ds(8 * z, 8)].astype(f32).reshape(256, B)
        srows[pl.ds(z * 256, 256), :] = s_ref[pl.ds(8 * z, 8)].astype(f32).reshape(256, B)
    grows[pl.ds(2048, 128), :] = jnp.zeros((128, B), f32)
    shifts[:, :, pl.ds(256, 128), :] = jnp.zeros((8, 4, 128, B), bf16)

    @pl.loop(0, 8)
    def _(c):
        shifted(grows, shifts, c)
        crows[pl.ds(c, 256, stride=8), :] = correlate(toep, shifts, c)

    for z in range(8):
        c_ref[pl.ds(8 * z, 8)] = crows[pl.ds(z * 256, 256), :].astype(bf16).reshape(8, 4, 8, B)
    for half in range(2):

        @pl.loop(0, HALF)
        def _(q):
            c = half * HALF + q
            saved_t = srows[pl.ds(c, 256, stride=8), :].T.astype(bf16)
            product_blocks(saved_t, shifts, blocks, c, q)

        fold(blocks, totals)
        for q in range(HALF):
            here = totals[pl.ds(64 * q, 64), pl.ds(B, B)]
            later = totals[pl.ds(64 * q, 64), pl.ds(0, B)]
            later = jnp.concatenate([later[1:], jnp.zeros((1, B), f32)], 0)
            d_ref[half * HALF + q] = here + later


def conv(f, g, s):
    length = f.shape[1]
    vm = pl.BlockSpec(memory_space=pltpu.VMEM)
    return pl.pallas_call(
        conv_kernel,
        out_shape=(jax.ShapeDtypeStruct(g.shape, bf16), jax.ShapeDtypeStruct((8, 64, B), f32)),
        in_specs=[vm] * 3,
        out_specs=(vm, vm),
        scratch_shapes=[
            pltpu.VMEM((8, length + B), f32),
            pltpu.VMEM((8, B, length), bf16),
            pltpu.VMEM((2048 + 128, B), f32),
            pltpu.VMEM((2048, B), f32),
            pltpu.VMEM((8, 4, 384, B), bf16),
            pltpu.VMEM((2048, B), f32),
            pltpu.VMEM((HALF * 64 * PITCH, B), f32),
            pltpu.VMEM((HALF * 64, 2 * B), f32),
        ],
        compiler_params=pltpu.CompilerParams(vmem_limit_bytes=60 << 20),
        name="conv",
    )(f, g, s)


def exchange(blocks, axes):
    return lax.all_to_all(blocks, axes, split_axis=0, concat_axis=0, tiled=True)


def shards(grad_output, post_gate, pre_gate, value_branch, long_filter, skip_weight):
    token_count = 4 * long_filter.shape[1]
    gated = (grad_output.astype(f32) * post_gate.astype(f32)).astype(bf16)
    saved = (pre_gate.astype(f32) * value_branch.astype(f32)).astype(bf16)
    own = lax.dynamic_slice_in_dim(long_filter, lax.axis_index("dp") * 8, 8, 0)
    axes = ("ctx", "dp")
    g = exchange(gated.reshape(256, 8, B), axes).reshape(64, 4, 8, B)
    s = exchange(saved.reshape(256, 8, B), axes).reshape(64, 4, 8, B)
    c, d = conv(own, g, s)
    back = exchange(c.reshape(256, 8, B), axes).reshape(1, 2048, B)
    d = d.reshape(8, 4, 2048).swapaxes(0, 1).reshape(32, 2048).astype(bf16)
    shares = lax.all_to_all(d, "dp", split_axis=0, concat_axis=0, tiled=True).astype(f32)
    summed = back.astype(f32) + skip_weight[None, :, None] * gated.astype(f32)
    return (
        (summed * value_branch.astype(f32)).astype(bf16),
        (summed * pre_gate.astype(f32)).astype(bf16),
        shares * (1.0 / math.sqrt(token_count)),
    )


def solution(mesh):
    return jax.shard_map(
        shards,
        mesh=mesh,
        in_specs=(P("dp", None, "ctx"),) * 4 + (P("ctx", None), P()),
        out_specs=(P("dp", None, "ctx"), P("dp", None, "ctx"), P("ctx", "dp")),
        check_vma=False,
    )
```

profile of v0, /device:TPU:1, one launch (start us, length us, event | category | flops | bytes accessed | tf_op | source)
XLA Modules:
  0.0 146.5 jit_solution(5994473129698590661)
XLA Ops:
  0.6 0.0 copy-start
  0.6 2.2 %fusion.4 = bf16[256,8,128]{2,1,0:T(8,128)(2,1)} fusion(bf16[1,2048,128]{2,1,0:T(8,128)(2,1)} %param.7, bf16[1,2048,128]{2,1,0:T(8,128)(2,1)} %param.6), kind=kLoop, calls=%fused_computation.12 | loop fusion | flops 1048576 | bytes 1572864 | tf_op jit(solution)/shard_map/reshape | solution.py:165
  2.9 0.0 copy-start.1
  2.9 0.0 copy-start.4
  2.9 15.7 %all-to-all-start = ((bf16[256,8,128]{2,1,0:T(8,128)(2,1)}), bf16[256,8,128]{2,1,0:T(8,128)(2,1)S(1)}, u32[]{:S(2)}, u32[]{:S(2)}) async-start(bf16[256,8,128]{2,1,0:T(8,128)(2,1)} %fusion.4), calls=%async_computation | async-start | bytes 1048576 | tf_op jit(solution)/shard_map/all_to_all | solution.py:156
  18.5 0.0 copy-done.1
  18.5 0.0 copy-done.4
  18.6 0.9 fusion.3
  19.5 20.5 %all-to-all-done = bf16[256,8,128]{2,1,0:T(8,128)(2,1)S(1)} async-done(((bf16[256,8,128]{2,1,0:T(8,128)(2,1)}), bf16[256,8,128]{2,1,0:T(8,128)(2,1)S(1)}, u32[]{:S(2)}, u32[]{:S(2)}) %all-to-all-start) | async-done | bytes 524320 | tf_op jit(solution)/shard_map/all_to_all | solution.py:156
  40.0 0.0 copy-start.5
  40.0 5.2 %all-to-all-start.1 = ((bf16[256,8,128]{2,1,0:T(8,128)(2,1)}), bf16[256,8,128]{2,1,0:T(8,128)(2,1)S(1)}, u32[]{:S(2)}, u32[]{:S(2)}) async-start(bf16[256,8,128]{2,1,0:T(8,128)(2,1)} %fusion.3), calls=%async_computation.1 | async-start | bytes 1048576 | tf_op jit(solution)/shard_map/all_to_all | solution.py:156
  45.2 0.0 copy-done.5
  45.2 0.0 copy-done
  45.2 0.7 constant_dynamic-slice_fusion.f_ref
  45.9 20.3 %all-to-all-done.1 = bf16[256,8,128]{2,1,0:T(8,128)(2,1)S(1)} async-done(((bf16[256,8,128]{2,1,0:T(8,128)(2,1)}), bf16[256,8,128]{2,1,0:T(8,128)(2,1)S(1)}, u32[]{:S(2)}, u32[]{:S(2)}) %all-to-all-start.1) | async-done | bytes 524320 | tf_op jit(solution)/shard_map/all_to_all | solution.py:156
  66.2 0.0 copy-start.6
  66.2 0.8 copy-done.6
  67.0 40.1 %conv.1 = (bf16[64,4,8,128]{3,2,1,0:T(8,128)(2,1)}, f32[8,64,128]{2,1,0:T(8,128)}) custom-call(f32[8,8192]{1,0:T(8,128)} %constant_dynamic-slice_fusion.f_ref, bf16[64,4,8,128]{3,2,1,0:T(8,128)(2,1)} %bitcast.16, bf16[64,4,8,128]{3,2,1,0:T(8,128)(2,1)} %bitcast.17), custom_call_target="tpu_custom_call" | custom-call | tf_op jit(solution)/shard_map/conv/pallas_call | solution.py:135
  107.1 1.0 convert_element_type.68
  108.2 0.1 copy.12
  108.2 7.3 %all_to_all.21 = bf16[4,8,2048]{2,1,0:T(8,128)(2,1)S(1)} all-to-all(bf16[4,8,2048]{2,1,0:T(8,128)(2,1)S(1)} %bitcast.19), channel_id=1, replica_groups=mesh['dp'=4,'ctx'=64] {'dp'}, dimensions={0} | all-to-all | bytes 262144 | tf_op jit(solution)/shard_map/all_to_all | solution.py:170
  115.5 0.0 copy-start.2
  115.5 0.0 copy-start.3
  115.5 7.8 %all-to-all-start.2 = ((bf16[256,8,128]{2,1,0:T(8,128)(2,1)}), bf16[256,8,128]{2,1,0:T(8,128)(2,1)}, u32[]{:S(2)}, u32[]{:S(2)}) async-start(bf16[256,8,128]{2,1,0:T(8,128)(2,1)} %bitcast.18), calls=%async_computation.2 | async-start | bytes 1048576 | tf_op jit(solution)/shard_map/all_to_all | solution.py:156
  123.3 0.0 copy-start.7
  123.3 0.7 multiply_bitcast_fusion
  124.0 20.0 %all-to-all-done.2 = bf16[256,8,128]{2,1,0:T(8,128)(2,1)} async-done(((bf16[256,8,128]{2,1,0:T(8,128)(2,1)}), bf16[256,8,128]{2,1,0:T(8,128)(2,1)}, u32[]{:S(2)}, u32[]{:S(2)}) %all-to-all-start.2) | async-done | bytes 524320 | tf_op jit(solution)/shard_map/all_to_all | solution.py:156
  144.0 0.0 copy-done.2
  144.0 0.0 copy-done.3
  144.0 0.0 copy-done.7
  144.0 2.5 %fusion = (bf16[1,2048,128]{2,1,0:T(8,128)(2,1)}, bf16[1,2048,128]{2,1,0:T(8,128)(2,1)}) fusion(bf16[1,2048,128]{2,1,0:T(8,128)(2,1)S(1)} %copy-done.1, bf16[256,8,128]{2,1,0:T(8,128)(2,1)} %all-to-all-done.2, f32[2048]{0:T(1024)S(1)} %copy-done.7, bf16[1,2048,128]{2,1,0:T(8,128)(2,1)S(1)} %copy-done.2, bf16[1,2048,128]{2,1,0:T(8,128)(2,1)S(1)} %copy-done.3, ...), kind=kLoop, calls=%fused_computation.3 | loop fusion | flops 3670016 | bytes 3678208 | tf_op jit(solution)/shard_map/convert_element_type | solution.py:174
  (1 shorter events, 0.0 us)
Async XLA Ops:
  0.6 44.6 %copy-start = (f32[32,8192]{1,0:T(8,128)S(1)}, f32[32,8192]{1,0:T(8,128)}, u32[]{:S(2)}) copy-start(f32[32,8192]{1,0:T(8,128)} %param.10) | copy-start | bytes 3145732
  2.9 15.7 %copy-start.1 = (bf16[1,2048,128]{2,1,0:T(8,128)(2,1)S(1)}, bf16[1,2048,128]{2,1,0:T(8,128)(2,1)}, u32[]{:S(2)}) copy-start(bf16[1,2048,128]{2,1,0:T(8,128)(2,1)} %param.8) | copy-start | bytes 1572868
  2.9 15.7 %copy-start.4 = (bf16[1,2048,128]{2,1,0:T(8,128)(2,1)S(1)}, bf16[1,2048,128]{2,1,0:T(8,128)(2,1)}, u32[]{:S(2)}) copy-start(bf16[1,2048,128]{2,1,0:T(8,128)(2,1)} %param.9) | copy-start | bytes 1572868
  2.9 37.1 %all-to-all-start = ((bf16[256,8,128]{2,1,0:T(8,128)(2,1)}), bf16[256,8,128]{2,1,0:T(8,128)(2,1)S(1)}, u32[]{:S(2)}, u32[]{:S(2)}) async-start(bf16[256,8,128]{2,1,0:T(8,128)(2,1)} %fusion.4), calls=%async_computation | async-start | bytes 1048576 | tf_op jit(solution)/shard_map/all_to_all | solution.py:156
  40.0 5.2 %copy-start.5 = (bf16[256,8,128]{2,1,0:T(8,128)(2,1)}, bf16[256,8,128]{2,1,0:T(8,128)(2,1)S(1)}, u32[]{:S(2)}) copy-start(bf16[256,8,128]{2,1,0:T(8,128)(2,1)S(1)} %all-to-all-done) | copy-start | bytes 1572868
  40.0 26.2 %all-to-all-start.1 = ((bf16[256,8,128]{2,1,0:T(8,128)(2,1)}), bf16[256,8,128]{2,1,0:T(8,128)(2,1)S(1)}, u32[]{:S(2)}, u32[]{:S(2)}) async-start(bf16[256,8,128]{2,1,0:T(8,128)(2,1)} %fusion.3), calls=%async_computation.1 | async-start | bytes 1048576 | tf_op jit(solution)/shard_map/all_to_all | solution.py:156
  66.2 0.8 copy-start.6
  115.5 28.5 %copy-start.2 = (bf16[1,2048,128]{2,1,0:T(8,128)(2,1)S(1)}, bf16[1,2048,128]{2,1,0:T(8,128)(2,1)}, u32[]{:S(2)}) copy-start(bf16[1,2048,128]{2,1,0:T(8,128)(2,1)} %param.7) | copy-start | bytes 1572868
  115.5 28.5 %copy-start.3 = (bf16[1,2048,128]{2,1,0:T(8,128)(2,1)S(1)}, bf16[1,2048,128]{2,1,0:T(8,128)(2,1)}, u32[]{:S(2)}) copy-start(bf16[1,2048,128]{2,1,0:T(8,128)(2,1)} %param.6) | copy-start | bytes 1572868
  115.5 28.5 %all-to-all-start.2 = ((bf16[256,8,128]{2,1,0:T(8,128)(2,1)}), bf16[256,8,128]{2,1,0:T(8,128)(2,1)}, u32[]{:S(2)}, u32[]{:S(2)}) async-start(bf16[256,8,128]{2,1,0:T(8,128)(2,1)} %bitcast.18), calls=%async_computation.2 | async-start | bytes 1048576 | tf_op jit(solution)/shard_map/all_to_all | solution.py:156
  123.3 20.7 %copy-start.7 = (f32[2048]{0:T(1024)S(1)}, f32[2048]{0:T(1024)}, u32[]{:S(2)}) copy-start(f32[2048]{0:T(1024)} %param.11) | copy-start | bytes 24580
where the time goes:
time: 147 us
  waiting for transfers between devices  60.8 us (41%)
  Pallas kernels  40.1 us (27%)
  starting transfers between devices  28.6 us (19%)
  other arithmetic  7.34 us (5%)
  blocking collectives  7.27 us (5%)
  local copies, waits for them, and re-layouts  1.67 us (1%)
    all_to_all x3, waiting for transfers between devices, exchange(): return lax.all_to_all(blocks, axes, split_axis=0, concat_axis=0, tiled=True)  60.8 us
    pallas_call x1, Pallas kernels, conv(): pl.pallas_call(conv_kernel, out_shape=(jax.ShapeDtypeStruct(g.shape, bf16...  40.1 us
    all_to_all x3, starting transfers between devices, exchange(): return lax.all_to_all(blocks, axes, split_axis=0, concat_axis=0, tiled=True)  28.6 us
    all_to_all x1, blocking collectives, shards(): lax.all_to_all(d, 'dp', split_axis=0, concat_axis=0, tiled=True).astype(f32)  7.27 us
  transfers between devices with their start and end apart: 3, of which 3 were waited for; matrix products, arithmetic and copies ran while one was open for 2% of the time, Pallas kernels for 0%

commit v1 on v0

--- a/solution.py
+++ b/solution.py
@@ -8,6 +8,9 @@
 from jax.experimental.pallas import tpu as pltpu
 from jax.sharding import PartitionSpec as P
 
+MESH = pl.DeviceIdType.MESH
+ORDER = (4, 3, 5, 6, 2, 7, 1, 0)
+GROUPS = ((0, 4), (4, 4))
 
 f32, bf16 = jnp.float32, jnp.bfloat16
 B = 128
@@ -27,10 +30,10 @@
     return v
 
 
-def build_filters(fpad, toep):
+def build_filters(fpad, toep, first, last):
     length = toep.shape[2]
 
-    @pl.loop(0, 8)
+    @pl.loop(first, last)
     def _(c):
         @pl.loop(0, length // W)
         def _(w):
@@ -95,49 +98,276 @@
         totals[...] += jnp.dot(jnp.concatenate(lhs, 1), jnp.concatenate(rhs, 0), preferred_element_type=f32)
 
 
-def conv_kernel(f_ref, g_ref, s_ref, c_ref, d_ref, fpad, toep, grows, srows, shifts, crows, blocks, totals):
+def wrap(v, n):
+    return jnp.where(v >= n, v - n, v)
+
+
+def kernel(
+    go_hbm, pg_hbm, pre_hbm, val_hbm, filt_hbm, skip_ref, gp_ref, gv_ref, taps_ref,
+    go, pg, pre, val, g_own, s_own, g_z, s_z, g_all, s_all, c_own, c_xy, c_z, t_own, t_all,
+    fpad, toep, grows, srows, shifts, crows, blocks, totals, trows, direct,
+    load_sem, z_send, z_recv, xy_send, xy_recv, t_send, t_recv,
+):
     length = toep.shape[2]
+    dp, ctx = lax.axis_index("dp"), lax.axis_index("ctx")
+    z = ctx // 8
+    plane = ctx - 8 * z
+    xl = plane // 4
+    y = plane - 4 * xl
+    xh = dp // 2
+    core = dp - 2 * xh
+    x = 2 * xh + xl
+    q = plane * 4 + dp
+
+    def z_peer(k, back):
+        step = ORDER[k] if back else (8 - ORDER[k]) % 8
+        return wrap(z + step, 8)
+
+    def each_xy_peer(body):
+        @pl.loop(0, 4)
+        def _(dy):
+            y2 = wrap(y + dy, 4)
+            for dx in range(4):
+                x2 = wrap(x + dx, 4)
+                xh2 = jnp.where(x2 >= 2, 1, 0)
+                plane2 = (x2 - 2 * xh2) * 4 + y2
+                for dc in range(2):
+                    core2 = wrap(core + dc, 2)
+                    dp2 = 2 * xh2 + core2
+                    if dx or dc:
+                        body(dp2, z * 8 + plane2, plane2 * 4 + dp2)
+                    else:
+
+                        @pl.when(dy > 0)
+                        def _():
+                            body(dp2, z * 8 + plane2, plane2 * 4 + dp2)
+
+    barrier = pltpu.get_barrier_semaphore()
+    for k in range(7):
+        pl.semaphore_signal(
+            barrier, inc=1, device_id=(dp, z_peer(k, False) * 8 + plane), device_id_type=MESH
+        )
+    each_xy_peer(
+        lambda d, c, q2: pl.semaphore_signal(barrier, inc=1, device_id=(d, c), device_id_type=MESH)
+    )
+    loads = [
+        pltpu.make_async_copy(a, b, load_sem.at[n])
+        for n, (a, b) in enumerate(
+            (
+                (go_hbm, go), (pg_hbm, pg), (pre_hbm, pre), (val_hbm, val),
+                (filt_hbm.at[pl.ds(pl.multiple_of(8 * dp, 8), 8)], fpad.at[:, pl.ds(B, length)]),
+            )
+        )
+    ]
+    for load in loads:
+        load.start()
+
+    def elementwise(a, b, out):
+        @pl.loop(0, 8)
+        def _(n):
+            rows = pl.ds(pl.multiple_of(n * 256, 256), 256)
+            prod = (a[rows, :].astype(f32) * b[rows, :].astype(f32)).astype(bf16)
+            out[n] = prod.reshape(32, 8, B)
+
+    def z_sends(src, dst, n):
+        return [
+            pltpu.make_async_remote_copy(
+                src_ref=src.at[z_peer(k, False)], dst_ref=dst.at[k],
+                send_sem=z_send.at[n, k], recv_sem=z_recv.at[n, k],
+                device_id=(dp, z_peer(k, False) * 8 + plane), device_id_type=MESH,
+            )
+            for k in range(7)
+        ]
+
+    def xy_start(src, dst, n, g, out):
+        lo, count = GROUPS[g]
+
+        def one(d, c, q2):
+            slots = pl.ds(lo, count)
+            pltpu.make_async_remote_copy(
+                src_ref=src.at[q2, slots] if out else src.at[slots, q2],
+                dst_ref=dst.at[q, slots],
+                send_sem=xy_send.at[n, g], recv_sem=xy_recv.at[n, g],
+                device_id=(d, c), device_id_type=MESH,
+            ).start()
+
+        each_xy_peer(one)
+
+    def xy_wait(src, dst, n, g, out, send):
+        slots = pl.ds(*GROUPS[g])
+        if send:
+            part = src.at[pl.ds(0, 31), slots] if out else src.at[slots, pl.ds(0, 31)]
+            pltpu.make_async_copy(part, part, xy_send.at[n, g]).wait()
+        else:
+            part = dst.at[pl.ds(0, 31), slots]
+            pltpu.make_async_copy(part, part, xy_recv.at[n, g]).wait()
+
+    loads[0].wait()
+    loads[1].wait()
+    elementwise(go, pg, g_own)
+    pl.semaphore_wait(barrier, 38)
+    g_sends = z_sends(g_own, g_z, 0)
+    for send in g_sends:
+        send.start()
+    g_z[7] = g_own[z]
+    loads[2].wait()
+    loads[3].wait()
+    elementwise(pre, val, s_own)
+    s_z[7] = s_own[z]
+    s_sends = z_sends(s_own, s_z, 1)
+
+    skip_t = skip_ref[...].T
+    for n in range(16):
+        part = g_own[n // 2, pl.ds(16 * (n % 2), 16)].astype(f32).reshape(B, B)
+        direct[pl.ds(n * B, B), :] = part * skip_t[:, n : n + 1]
+
+    loads[4].wait()
     fpad[:, :B] = jnp.zeros((8, B), f32)
-    fpad[:, pl.ds(B, length)] = f_ref[...]
-    build_filters(fpad, toep)
-    for z in range(8):
-        grows[pl.ds(z * 256, 256), :] = g_ref[pl.ds(8 * z, 8)].astype(f32).reshape(256, B)
-        srows[pl.ds(z * 256, 256), :] = s_ref[pl.ds(8 * z, 8)].astype(f32).reshape(256, B)
     grows[pl.ds(2048, 128), :] = jnp.zeros((128, B), f32)
     shifts[:, :, pl.ds(256, 128), :] = jnp.zeros((8, 4, 128, B), bf16)
+    build_filters(fpad, toep, 0, 3)
+    for k in range(4):
+        g_sends[k].wait_recv()
+    xy_start(g_z, g_all, 0, 0, False)
+    for send in s_sends:
+        send.start()
+    build_filters(fpad, toep, 3, 4)
+    for k in range(4, 7):
+        g_sends[k].wait_recv()
+    xy_start(g_z, g_all, 0, 1, False)
+    for k in range(8):
+        g_all[q, k] = g_z[k, q]
+    build_filters(fpad, toep, 4, 8)
+
+    def unpack(slabs, rows):
+        for k in range(8):
+            there = wrap(z + ORDER[k], 8)
+            rows[pl.ds(pl.multiple_of(there * 256, 256), 256), :] = (
+                slabs[:, k].astype(f32).reshape(256, B)
+            )
+
+    xy_wait(g_z, g_all, 0, 0, False, False)
+    xy_wait(g_z, g_all, 0, 1, False, False)
+    unpack(g_all, grows)
 
     @pl.loop(0, 8)
     def _(c):
         shifted(grows, shifts, c)
         crows[pl.ds(c, 256, stride=8), :] = correlate(toep, shifts, c)
 
-    for z in range(8):
-        c_ref[pl.ds(8 * z, 8)] = crows[pl.ds(z * 256, 256), :].astype(bf16).reshape(8, 4, 8, B)
+    for k in range(8):
+        there = wrap(z + ORDER[k], 8)
+        c_own[:, k] = (
+            crows[pl.ds(pl.multiple_of(there * 256, 256), 256), :].astype(bf16).reshape(32, 8, B)
+        )
+    xy_start(c_own, c_xy, 2, 0, True)
+    xy_start(c_own, c_xy, 2, 1, True)
+    for k in range(8):
+        c_xy[q, k] = c_own[q, k]
+
+    for k in range(4):
+        s_sends[k].wait_recv()
+    xy_start(s_z, s_all, 1, 0, False)
+    for k in range(4, 7):
+        s_sends[k].wait_recv()
+    xy_start(s_z, s_all, 1, 1, False)
+    for k in range(8):
+        s_all[q, k] = s_z[k, q]
+
+    c_sends = [
+        pltpu.make_async_remote_copy(
+            src_ref=c_xy.at[:, k], dst_ref=c_z.at[k],
+            send_sem=z_send.at[2, k], recv_sem=z_recv.at[2, k],
+            device_id=(dp, z_peer(k, True) * 8 + plane), device_id_type=MESH,
+        )
+        for k in range(7)
+    ]
+    for g in range(2):
+        xy_wait(c_own, c_xy, 2, g, True, False)
+        for k in range(GROUPS[g][0], min(7, sum(GROUPS[g]))):
+            c_sends[k].start()
+    c_z[7] = c_xy[:, 7]
+
+    xy_wait(s_z, s_all, 1, 0, False, False)
+    xy_wait(s_z, s_all, 1, 1, False, False)
+    unpack(s_all, srows)
     for half in range(2):
 
         @pl.loop(0, HALF)
-        def _(q):
-            c = half * HALF + q
+        def _(n):
+            c = half * HALF + n
             saved_t = srows[pl.ds(c, 256, stride=8), :].T.astype(bf16)
-            product_blocks(saved_t, shifts, blocks, c, q)
+            product_blocks(saved_t, shifts, blocks, c, n)
 
         fold(blocks, totals)
-        for q in range(HALF):
-            here = totals[pl.ds(64 * q, 64), pl.ds(B, B)]
-            later = totals[pl.ds(64 * q, 64), pl.ds(0, B)]
+        for n in range(HALF):
+            here = totals[pl.ds(64 * n, 64), pl.ds(B, B)]
+            later = totals[pl.ds(64 * n, 64), pl.ds(0, B)]
             later = jnp.concatenate([later[1:], jnp.zeros((1, B), f32)], 0)
-            d_ref[half * HALF + q] = here + later
-
-
-def conv(f, g, s):
-    length = f.shape[1]
+            trows[pl.ds(half * HALF + n, 64, stride=8), :] = here + later
+
+    for p in range(4):
+        t_own[p] = trows[pl.ds(128 * p, 128), :].astype(bf16).reshape(16, 8, B)
+    t_sends = []
+    for s in range(1, 4):
+        p = wrap(dp + s, 4)
+        t_sends.append(
+            pltpu.make_async_remote_copy(
+                src_ref=t_own.at[p], dst_ref=t_all.at[s],
+                send_sem=t_send.at[s - 1], recv_sem=t_recv.at[s - 1],
+                device_id=(p, ctx), device_id_type=MESH,
+            )
+        )
+        t_sends[-1].start()
+    t_all[0] = t_own[dp]
+
+    for k in (7, 0, 1, 2, 3, 4, 5, 6):
+        if k < 7:
+            c_sends[k].wait_recv()
+        rows = pl.ds(pl.multiple_of(z_peer(k, False) * 256, 256), 256)
+        summed = c_z[k].astype(f32).reshape(256, B) + direct[rows, :]
+        gp_ref[rows, :] = (summed * val[rows, :].astype(f32)).astype(bf16)
+        gv_ref[rows, :] = (summed * pre[rows, :].astype(f32)).astype(bf16)
+
+    scale = 1.0 / math.sqrt(4 * length)
+    for s in range(4):
+        if s:
+            t_sends[s - 1].wait_recv()
+        rows = pl.ds(pl.multiple_of(8 * wrap(dp + (4 - s) % 4, 4), 8), 8)
+        for m in range(16):
+            taps_ref[rows, pl.ds(m * B, B)] = t_all[s, m].astype(f32) * scale
+
+    for send in g_sends + s_sends + c_sends + t_sends:
+        send.wait_send()
+    for g in range(2):
+        xy_wait(g_z, g_all, 0, g, False, True)
+        xy_wait(s_z, s_all, 1, g, False, True)
+        xy_wait(c_own, c_xy, 2, g, True, True)
+
+
+def shards(grad_output, post_gate, pre_gate, value_branch, long_filter, skip_weight):
+    channels, length = skip_weight.shape[0], long_filter.shape[1]
     vm = pl.BlockSpec(memory_space=pltpu.VMEM)
-    return pl.pallas_call(
-        conv_kernel,
-        out_shape=(jax.ShapeDtypeStruct(g.shape, bf16), jax.ShapeDtypeStruct((8, 64, B), f32)),
-        in_specs=[vm] * 3,
-        out_specs=(vm, vm),
-        scratch_shapes=[
+    own = pltpu.VMEM((channels, B), bf16)
+    by_z = pltpu.VMEM((8, 32, 8, B), bf16)
+    by_q = pltpu.VMEM((32, 8, 8, B), bf16)
+    by_p = pltpu.VMEM((4, 16, 8, B), bf16)
+    dma = pltpu.SemaphoreType.DMA
+    gp, gv, taps = pl.pallas_call(
+        kernel,
+        out_shape=(
+            jax.ShapeDtypeStruct((channels, B), bf16),
+            jax.ShapeDtypeStruct((channels, B), bf16),
+            jax.ShapeDtypeStruct((32, length // 4), f32),
+        ),
+        in_specs=[pl.BlockSpec(memory_space=pl.ANY)] * 5 + [vm],
+        out_specs=(vm, vm, vm),
+        scratch_shapes=[own] * 4
+        + [by_z] * 4
+        + [by_q] * 4
+        + [by_z]
+        + [by_p] * 2
+        + [
             pltpu.VMEM((8, length + B), f32),
             pltpu.VMEM((8, B, length), bf16),
             pltpu.VMEM((2048 + 128, B), f32),
@@ -146,34 +376,25 @@
             pltpu.VMEM((2048, B), f32),
             pltpu.VMEM((HALF * 64 * PITCH, B), f32),
             pltpu.VMEM((HALF * 64, 2 * B), f32),
+            pltpu.VMEM((512, B), f32),
+            pltpu.VMEM((2048, B), f32),
+            dma((5,)),
+            dma((3, 7)),
+            dma((3, 7)),
+            dma((3, 2)),
+            dma((3, 2)),
+            dma((3,)),
+            dma((3,)),
         ],
-        compiler_params=pltpu.CompilerParams(vmem_limit_bytes=60 << 20),
-        name="conv",
-    )(f, g, s)
-
-
-def exchange(blocks, axes):
-    return lax.all_to_all(blocks, axes, split_axis=0, concat_axis=0, tiled=True)
-
-
-def shards(grad_output, post_gate, pre_gate, value_branch, long_filter, skip_weight):
-    token_count = 4 * long_filter.shape[1]
-    gated = (grad_output.astype(f32) * post_gate.astype(f32)).astype(bf16)
-    saved = (pre_gate.astype(f32) * value_branch.astype(f32)).astype(bf16)
-    own = lax.dynamic_slice_in_dim(long_filter, lax.axis_index("dp") * 8, 8, 0)
-    axes = ("ctx", "dp")
-    g = exchange(gated.reshape(256, 8, B), axes).reshape(64, 4, 8, B)
-    s = exchange(saved.reshape(256, 8, B), axes).reshape(64, 4, 8, B)
-    c, d = conv(own, g, s)
-    back = exchange(c.reshape(256, 8, B), axes).reshape(1, 2048, B)
-    d = d.reshape(8, 4, 2048).swapaxes(0, 1).reshape(32, 2048).astype(bf16)
-    shares = lax.all_to_all(d, "dp", split_axis=0, concat_axis=0, tiled=True).astype(f32)
-    summed = back.astype(f32) + skip_weight[None, :, None] * gated.astype(f32)
-    return (
-        (summed * value_branch.astype(f32)).astype(bf16),
-        (summed * pre_gate.astype(f32)).astype(bf16),
-        shares * (1.0 / math.sqrt(token_count)),
+        compiler_params=pltpu.CompilerParams(
+            collective_id=0, has_side_effects=True, vmem_limit_bytes=62 << 20
+        ),
+        name="hyena",
+    )(
+        grad_output[0], post_gate[0], pre_gate[0], value_branch[0], long_filter,
+        skip_weight.reshape(16, B),
     )
+    return gp[None], gv[None], taps
 
 
 def solution(mesh):

time: 147 us -> 82 us (0.56)
  waiting for transfers between devices: 60.8 us -> 0 us
  Pallas kernels: 40.1 us -> 77.4 us
  starting transfers between devices: 28.6 us -> 0 us
  other arithmetic: 7.34 us -> 0 us
  blocking collectives: 7.27 us -> 0 us
  local copies, waits for them, and re-layouts: 1.67 us -> 3.72 us
    all_to_all x3 -> x0, waiting for transfers between devices: 60.8 us -> none  [exchange(): return lax.all_to_all(blocks, axes, split_axis=0, concat_axis=0, tiled=True)]
    pallas_call x1, Pallas kernels: 40.1 us -> 77.4 us  [shards(): pl.pallas_call(kernel, out_shape=(jax.ShapeDtypeStruct((channels, B), bf1...]
    all_to_all x3 -> x0, starting transfers between devices: 28.6 us -> none  [exchange(): return lax.all_to_all(blocks, axes, split_axis=0, concat_axis=0, tiled=True)]
    all_to_all x1 -> x0, blocking collectives: 7.27 us -> none  [shards(): lax.all_to_all(d, 'dp', split_axis=0, concat_axis=0, tiled=True).astype(f32)]
    convert_element_type x2 -> x0, other arithmetic: 3.46 us -> none  [the longest x1 2.49 us: shards(): (summed * pre_gate.astype(f32)).astype(bf16)]
    reshape x2 -> x0, other arithmetic: 3.15 us -> none  [the longest x1 2.22 us: shards(): g = exchange(gated.reshape(256, 8, B), axes).reshape(64, 4, 8, B)]
    unnamed x16 -> x7, local copies, waits for them, and re-layouts: 0.83 us -> 3.72 us
  transfers between devices with their start and end apart: 3 -> 0, of which waited for: 3 -> 0; matrix products, arithmetic and copies ran while one was open for 2% -> 0% of each run, Pallas kernels for 0% -> 0%
where the time goes in v1:
time: 82 us; the launch traced here: 81.8 us
  Pallas kernels  77.4 us (94%)
  local copies, waits for them, and re-layouts  3.72 us (5%)
    pallas_call x1, Pallas kernels, shards(): pl.pallas_call(kernel, out_shape=(jax.ShapeDtypeStruct((channels, B), bf1...  77.4 us
    unnamed x7, local copies, waits for them, and re-layouts  3.72 us

profile of v1, /device:TPU:1, one launch (start us, length us, event | category | flops | bytes accessed | tf_op | source)
XLA Modules:
  0.0 81.8 jit_solution(1892992298709502744)
XLA Ops:
  0.6 77.4 %hyena.1 = (bf16[2048,128]{1,0:T(8,128)(2,1)}, bf16[2048,128]{1,0:T(8,128)(2,1)}, f32[32,2048]{1,0:T(8,128)}) custom-call(bf16[2048,128]{1,0:T(8,128)(2,1)} %bitcast.9, bf16[2048,128]{1,0:T(8,128)(2,1)} %bitcast.10, bf16[2048,128]{1,0:T(8,128)(2,1)} %bitcast.11, bf16[2048,128]{1,0:T(8,128)(2,1)} %bitcast.12, f32[32,8192]{1,0:T(8,128)} %filt_hbm.1, ...), custom_call_target="tpu_custom_call" | custom-call | tf_op jit(solution)/shard_map/hyena/pallas_call | solution.py:356
  78.1 0.0 copy-start
  78.1 1.9 %copy.12 = bf16[1,2048,128]{2,1,0:T(8,128)(2,1)} copy(bf16[1,2048,128]{2,1,0:T(8,128)(2,1)} %bitcast.8) | data formatting | bytes 1048576
  80.0 0.0 copy-done
  80.0 0.0 copy-start.1
  80.0 0.8 copy.13
  80.8 0.3 copy-done.1
  81.1 0.7 copy.14
Async XLA Ops:
  78.1 1.9 %copy-start = (bf16[2048,128]{1,0:T(8,128)(2,1)S(1)}, bf16[2048,128]{1,0:T(8,128)(2,1)}, u32[]{:S(2)}) copy-start(bf16[2048,128]{1,0:T(8,128)(2,1)} %get-tuple-element.7) | copy-start | bytes 1572868
  80.0 1.1 %copy-start.1 = (f32[32,2048]{1,0:T(8,128)S(1)}, f32[32,2048]{1,0:T(8,128)}, u32[]{:S(2)}) copy-start(f32[32,2048]{1,0:T(8,128)} %get-tuple-element.14) | copy-start | bytes 786436

commit v2 on v1

v2 whole, which is shorter than its diff:
```python
import functools
import math

import jax
import jax.numpy as jnp
from jax import lax
from jax.experimental import pallas as pl
from jax.experimental.pallas import tpu as pltpu
from jax.sharding import PartitionSpec as P

MESH = pl.DeviceIdType.MESH
ORDER = (4, 3, 5, 6, 2, 7, 1, 0)
AHEAD = 2

f32, bf16 = jnp.float32, jnp.bfloat16
B = 128
W = 2048


def row_bits(shape):
    return lax.broadcasted_iota(jnp.int32, shape, 0)


def stagger(v, left):
    width = v.shape[1]
    rows = row_bits(v.shape)
    for bit in (1, 2, 4):
        moved = pltpu.roll(v, (width - bit) if left else bit, 1)
        v = jnp.where((rows & bit) != 0, moved, v)
    return v


def build_filters(fpad, toep, first, last):
    length = toep.shape[2]

    @pl.loop(first, last)
    def _(c):
        @pl.loop(0, length // W)
        def _(w):
            lanes = pl.ds(pl.multiple_of(w * W, W), W + B)
            v = jnp.broadcast_to(fpad[pl.ds(c, 1), lanes], (8, W + B))
            v = stagger(v, False)
            for a in range(0, 16, 2):
                lo = v if a == 0 else pltpu.roll(v, 8 * a, 1)
                hi = pltpu.roll(v, 8 * a + 8, 1)
                both = jnp.concatenate([lo[:, B:], hi[:, B:]], 0).astype(bf16)
                toep[c, pl.ds(8 * a, 16), pl.ds(pl.multiple_of(w * W, W), W)] = both


def shifted(rows, out, c):
    for p in range(4):
        out[c, p, pl.ds(0, 256), :] = rows[pl.ds(c + 32 * p, 256, stride=8), :].astype(bf16)


def correlate(toep, shifts, c):
    acc = jnp.zeros((256, B), f32)
    for d4 in range(16):
        live = 256 - 16 * d4
        part = jnp.zeros((live, B), f32)
        for h in range(2):
            lhs = jnp.concatenate([shifts[c, 2 * h + e, pl.ds(16 * d4, live), :] for e in range(2)], 1)
            rhs = toep[c, :, pl.ds((4 * d4 + 2 * h) * B, 2 * B)]
            part += lax.dot_general(lhs, rhs, (((1,), (1,)), ((), ())), preferred_element_type=f32)
        if live == 256:
            acc += part
        else:
            acc = jnp.concatenate([acc[:live] + part, acc[live:]], 0)
    return acc


PITCH = 136
HALF = 4

def product_blocks(saved_t, shifts, blocks, c, slot):
    for d4 in range(16):
        depth = 256 if d4 < 8 else 128
        for h in range(2):
            m = 4 * d4 + 2 * h
            rhs = jnp.concatenate([shifts[c, 2 * h + e, pl.ds(16 * d4, depth), :] for e in range(2)], 1)
            out = jnp.dot(saved_t[:, :depth], rhs, preferred_element_type=f32)
            for e in range(2):
                blocks[pl.ds(pl.multiple_of((slot * 64 + m + e) * PITCH, 8), B), :] = out[:, e * B:(e + 1) * B]

def fold(blocks, totals, step=16):
    totals[...] = jnp.zeros(totals.shape, f32)
    rows = totals.shape[0]
    k = lax.broadcasted_iota(jnp.int32, (B, 2 * B), 0)
    n = lax.broadcasted_iota(jnp.int32, (B, 2 * B), 1)
    gap = n - k - B

    @pl.loop(0, B // step)
    def _(t):
        lhs, rhs = [], []
        for e in range(step):
            jp = t * step + e
            lhs.append(blocks[pl.ds(jp, rows, stride=PITCH), :].astype(bf16))
            rhs.append(jnp.where(gap == -jp, 1.0, 0.0).astype(bf16))
        totals[...] += jnp.dot(jnp.concatenate(lhs, 1), jnp.concatenate(rhs, 0), preferred_element_type=f32)


def wrap(v, n):
    return jnp.where(v >= n, v - n, v)


def kernel(
    go_hbm, pg_hbm, pre_hbm, val_hbm, filt_hbm, back_ref, taps_ref,
    go, pg, pre, val, g_own, s_own, g_z, s_z, g_all, s_all, c_own, c_xy, c_z, t_own, t_all,
    fpad, toep, grows, srows, shifts, crows, blocks, totals, trows,
    load_sem, z_send, z_recv, xy_send, xy_recv, c_recv, t_send, t_recv,
):
    length = toep.shape[2]
    dp, ctx = lax.axis_index("dp"), lax.axis_index("ctx")
    z = ctx // 8
    plane = ctx - 8 * z
    xl = plane // 4
    y = plane - 4 * xl
    xh = dp // 2
    core = dp - 2 * xh
    x = 2 * xh + xl
    q = plane * 4 + dp
    member = plane * 2 + xh

    loads = [
        pltpu.make_async_copy(a, b, load_sem.at[n])
        for n, (a, b) in enumerate(
            (
                (go_hbm, go), (pg_hbm, pg), (pre_hbm, pre), (val_hbm, val),
                (filt_hbm.at[pl.ds(pl.multiple_of(8 * dp, 8), 8)], fpad.at[:, pl.ds(B, length)]),
            )
        )
    ]
    for load in loads:
        load.start()

    def z_peer(k, back):
        step = ORDER[k] if back else (8 - ORDER[k]) % 8
        return wrap(z + step, 8)

    def chip(x2, y2):
        xh2 = jnp.where(x2 >= 2, 1, 0)
        return (x2 - 2 * xh2) * 4 + y2, xh2

    def each_xy_peer(body):
        @pl.loop(0, 4)
        def _(dy):
            y2 = wrap(y + dy, 4)
            for dx in range(4):
                plane2, xh2 = chip(wrap(x + dx, 4), y2)
                for dc in range(2):
                    dp2 = 2 * xh2 + wrap(core + dc, 2)
                    if dx or dc:
                        body(dp2, z * 8 + plane2, plane2 * 4 + dp2)
                    else:

                        @pl.when(dy > 0)
                        def _():
                            body(dp2, z * 8 + plane2, plane2 * 4 + dp2)

    barrier = pltpu.get_barrier_semaphore()
    for k in range(7):
        pl.semaphore_signal(
            barrier, inc=1, device_id=(dp, z_peer(k, False) * 8 + plane), device_id_type=MESH
        )
    each_xy_peer(
        lambda d, c, q2: pl.semaphore_signal(barrier, inc=1, device_id=(d, c), device_id_type=MESH)
    )

    def elementwise(a, b, out):
        @pl.loop(0, 8)
        def _(there):
            rows = pl.ds(pl.multiple_of(there * 256, 256), 256)
            prod = (a[rows, :].astype(f32) * b[rows, :].astype(f32)).reshape(16, 2, 8, B)
            for n in range(2):
                out[n, there] = prod[:, n].astype(bf16)

    def z_sends(src, dst, t, n):
        return [
            pltpu.make_async_remote_copy(
                src_ref=src.at[n, z_peer(k, False)], dst_ref=dst.at[n, k],
                send_sem=z_send.at[t, n, k], recv_sem=z_recv.at[t, n, k],
                device_id=(dp, z_peer(k, False) * 8 + plane), device_id_type=MESH,
            )
            for k in range(7)
        ]

    def spread(src, dst, t, n):
        @pl.loop(0, 4)
        def _(dy):
            y2 = wrap(y + dy, 4)
            for dx in range(4):
                plane2, xh2 = chip(wrap(x + dx, 4), y2)
                copy = pltpu.make_async_remote_copy(
                    src_ref=src.at[n, :, plane2 * 2 + xh2], dst_ref=dst.at[q],
                    send_sem=xy_send.at[t], recv_sem=xy_recv.at[t],
                    device_id=(2 * xh2 + n, z * 8 + plane2), device_id_type=MESH,
                )
                if dx:
                    copy.start()
                else:
                    pl.when((dy > 0) | (core != n))(copy.start)

    def wait_31(ref, sem):
        part = ref.at[pl.ds(0, 31)]
        pltpu.make_async_copy(part, part, sem).wait()

    loads[0].wait()
    loads[1].wait()
    elementwise(go, pg, g_own)
    pl.semaphore_wait(barrier, 38)
    g_sends = [z_sends(g_own, g_z, 0, n) for n in range(2)]
    s_sends = [z_sends(s_own, s_z, 1, n) for n in range(2)]
    queue = g_sends + s_sends

    def launch(n):
        if n < 4:
            for send in queue[n]:
                send.start()

    def forward(n):
        for send in queue[n]:
            send.wait_recv()
        launch(n + AHEAD)
        if n < 2:
            spread(g_z, g_all, 0, n)
        else:
            spread(s_z, s_all, 1, n - 2)

    for n in range(AHEAD):
        launch(n)
    for n in range(2):
        g_z[n, 7] = g_own[n, z]
    loads[2].wait()
    loads[3].wait()
    elementwise(pre, val, s_own)
    for n in range(2):
        s_z[n, 7] = s_own[n, z]

    loads[4].wait()
    fpad[:, :B] = jnp.zeros((8, B), f32)
    grows[pl.ds(2048, 128), :] = jnp.zeros((128, B), f32)
    shifts[:, :, pl.ds(256, 128), :] = jnp.zeros((8, 4, 128, B), bf16)
    build_filters(fpad, toep, 0, 3)
    forward(0)
    build_filters(fpad, toep, 3, 6)
    forward(1)
    g_all[q] = g_z[core, :, member]
    build_filters(fpad, toep, 6, 8)

    def unpack(slabs, rows):
        for k in range(8):
            there = wrap(z + ORDER[k], 8)
            rows[pl.ds(pl.multiple_of(there * 256, 256), 256), :] = (
                slabs[:, k].astype(f32).reshape(256, B)
            )

    wait_31(g_all, xy_recv.at[0])
    unpack(g_all, grows)

    def correlations(first, last):
        @pl.loop(first, last)
        def _(c):
            shifted(grows, shifts, c)
            crows[pl.ds(c, 256, stride=8), :] = correlate(toep, shifts, c)

    correlations(0, 3)
    forward(2)
    correlations(3, 6)
    forward(3)
    s_all[q] = s_z[core, :, member]
    correlations(6, 8)

    for k in range(8):
        there = wrap(z + ORDER[k], 8)
        c_own[:, k] = (
            crows[pl.ds(pl.multiple_of(there * 256, 256), 256), :].astype(bf16).reshape(32, 8, B)
        )

    def back(d, c, q2):
        pltpu.make_async_remote_copy(
            src_ref=c_own.at[q2], dst_ref=c_xy.at[core, member],
            send_sem=xy_send.at[2], recv_sem=c_recv.at[core],
            device_id=(d, c), device_id_type=MESH,
        ).start()

    each_xy_peer(back)
    c_xy[core, member] = c_own[q]

    c_sends = [
        pltpu.make_async_remote_copy(
            src_ref=c_xy.at[n, :, k], dst_ref=c_z.at[k, n],
            send_sem=z_send.at[2, n, k], recv_sem=z_recv.at[2, n, k],
            device_id=(dp, z_peer(k, True) * 8 + plane), device_id_type=MESH,
        )
        for n in range(2)
        for k in range(7)
    ]

    def part_wait(n, count):
        part = c_xy.at[n, pl.ds(0, count)]
        pltpu.make_async_copy(part, part, c_recv.at[n]).wait()

    def send_back(n):
        pl.when(core == n)(lambda: part_wait(n, 15))
        pl.when(core != n)(lambda: part_wait(n, 16))
        for send in c_sends[7 * n : 7 * n + 7]:
            send.start()
        c_z[7, n] = c_xy[n, :, 7]

    def multiply(first, last, base):
        @pl.loop(first, last)
        def _(c):
            saved_t = srows[pl.ds(c, 256, stride=8), :].T.astype(bf16)
            product_blocks(saved_t, shifts, blocks, c, c - base)

    def sum_up(base):
        fold(blocks, totals)
        for n in range(HALF):
            here = totals[pl.ds(64 * n, 64), pl.ds(B, B)]
            later = totals[pl.ds(64 * n, 64), pl.ds(0, B)]
            later = jnp.concatenate([later[1:], jnp.zeros((1, B), f32)], 0)
            trows[pl.ds(base + n, 64, stride=8), :] = here + later

    wait_31(s_all, xy_recv.at[1])
    unpack(s_all, srows)
    multiply(0, 3, 0)
    send_back(0)
    multiply(3, 4, 0)
    send_back(1)
    sum_up(0)
    multiply(4, 8, 4)
    sum_up(4)

    for p in range(4):
        t_own[p] = trows[pl.ds(128 * p, 128), :].astype(bf16).reshape(16, 8, B)
    t_sends = []
    for s in range(1, 4):
        p = wrap(dp + s, 4)
        t_sends.append(
            pltpu.make_async_remote_copy(
                src_ref=t_own.at[p], dst_ref=t_all.at[s],
                send_sem=t_send.at[s - 1], recv_sem=t_recv.at[s - 1],
                device_id=(p, ctx), device_id_type=MESH,
            )
        )
        t_sends[-1].start()
    t_all[0] = t_own[dp]

    for send in c_sends:
        send.wait_recv()
    for k in range(8):
        for n in range(2):
            for m in range(16):
                back_ref[z_peer(k, False), 2 * m + n] = c_z[k, n, m]

    for s in range(4):
        if s:
            t_sends[s - 1].wait_recv()
        rows = pl.ds(pl.multiple_of(8 * wrap(dp + (4 - s) % 4, 4), 8), 8)
        for m in range(16):
            taps_ref[rows, pl.ds(m * B, B)] = t_all[s, m].astype(f32)

    for send in sum(queue, []) + c_sends + t_sends:
        send.wait_send()
    wait_31(g_all, xy_send.at[0])
    wait_31(s_all, xy_send.at[1])
    wait_31(c_own, xy_send.at[2])


def shards(grad_output, post_gate, pre_gate, value_branch, long_filter, skip_weight):
    channels, length = skip_weight.shape[0], long_filter.shape[1]
    vm = pl.BlockSpec(memory_space=pltpu.VMEM)
    own = pltpu.VMEM((channels, B), bf16)
    by_class = pltpu.VMEM((2, 8, 16, 8, B), bf16)
    by_q = pltpu.VMEM((32, 8, 8, B), bf16)
    by_p = pltpu.VMEM((4, 16, 8, B), bf16)
    dma = pltpu.SemaphoreType.DMA
    back, taps = pl.pallas_call(
        kernel,
        out_shape=(
            jax.ShapeDtypeStruct((8, 32, 8, B), bf16),
            jax.ShapeDtypeStruct((32, length // 4), f32),
        ),
        in_specs=[pl.BlockSpec(memory_space=pl.ANY)] * 5,
        out_specs=(vm, vm),
        scratch_shapes=[own] * 4
        + [by_class] * 4
        + [by_q] * 3
        + [pltpu.VMEM((2, 16, 8, 8, B), bf16), pltpu.VMEM((8, 2, 16, 8, B), bf16)]
        + [by_p] * 2
        + [
            pltpu.VMEM((8, length + B), f32),
            pltpu.VMEM((8, B, length), bf16),
            pltpu.VMEM((2048 + 128, B), f32),
            pltpu.VMEM((2048, B), f32),
            pltpu.VMEM((8, 4, 384, B), bf16),
            pltpu.VMEM((2048, B), f32),
            pltpu.VMEM((HALF * 64 * PITCH, B), f32),
            pltpu.VMEM((HALF * 64, 2 * B), f32),
            pltpu.VMEM((512, B), f32),
            dma((5,)),
            dma((3, 2, 7)),
            dma((3, 2, 7)),
            dma((3,)),
            dma((2,)),
            dma((2,)),
            dma((3,)),
            dma((3,)),
        ],
        compiler_params=pltpu.CompilerParams(
            collective_id=0, has_side_effects=True, vmem_limit_bytes=62 << 20
        ),
        name="hyena",
    )(grad_output[0], post_gate[0], pre_gate[0], value_branch[0], long_filter)
    gated = (grad_output.astype(f32) * post_gate.astype(f32)).astype(bf16)
    summed = back.reshape(1, channels, B).astype(f32) + skip_weight[None, :, None] * gated.astype(f32)
    return (
        (summed * value_branch.astype(f32)).astype(bf16),
        (summed * pre_gate.astype(f32)).astype(bf16),
        taps * (1.0 / math.sqrt(4 * length)),
    )


def solution(mesh):
    return jax.shard_map(
        shards,
        mesh=mesh,
        in_specs=(P("dp", None, "ctx"),) * 4 + (P("ctx", None), P()),
        out_specs=(P("dp", None, "ctx"), P("dp", None, "ctx"), P("ctx", "dp")),
        check_vma=False,
    )
```

time: 82 us -> 71.8 us (0.88)
  Pallas kernels: 77.4 us -> 66.7 us
  other arithmetic: 0 us -> 4.23 us
  local copies, waits for them, and re-layouts: 3.72 us -> 0.02 us
    pallas_call x1, Pallas kernels: 77.4 us -> 66.7 us  [shards(): pl.pallas_call(kernel, out_shape=(jax.ShapeDtypeStruct((8, 32, 8, B), bf1...]
    unnamed x7 -> x10, local copies, waits for them, and re-layouts: 3.72 us -> 0.02 us
    convert_element_type x0 -> x1, other arithmetic: none -> 2.5 us  [shards(): (summed * pre_gate.astype(f32)).astype(bf16)]
    mul x0 -> x1, other arithmetic: none -> 1.73 us  [shards(): taps * (1.0 / math.sqrt(4 * length))]
where the time goes in v2:
time: 71.8 us; the launch traced here: 71.6 us
  Pallas kernels  66.7 us (93%)
  other arithmetic  4.23 us (6%)
    pallas_call x1, Pallas kernels, shards(): pl.pallas_call(kernel, out_shape=(jax.ShapeDtypeStruct((8, 32, 8, B), bf1...  66.7 us
    convert_element_type x1, other arithmetic, shards(): (summed * pre_gate.astype(f32)).astype(bf16)  2.5 us
    mul x1, other arithmetic, shards(): taps * (1.0 / math.sqrt(4 * length))  1.73 us

profile of v2, /device:TPU:1, one launch (start us, length us, event | category | flops | bytes accessed | tf_op | source)
XLA Modules:
  0.0 71.6 jit_solution(12203461257390152270)
XLA Ops:
  0.6 0.0 copy-start.1
  0.6 0.0 copy-start.2
  0.7 0.0 copy-start.3
  0.7 0.0 copy-start.4
  0.7 66.7 %hyena.1 = (bf16[8,32,8,128]{3,2,1,0:T(8,128)(2,1)}, f32[32,2048]{1,0:T(8,128)}) custom-call(bf16[2048,128]{1,0:T(8,128)(2,1)} %bitcast.7, bf16[2048,128]{1,0:T(8,128)(2,1)} %bitcast.8, bf16[2048,128]{1,0:T(8,128)(2,1)} %bitcast.6, bf16[2048,128]{1,0:T(8,128)(2,1)} %bitcast.9, f32[32,8192]{1,0:T(8,128)} %filt_hbm.1), custom_call_target="tpu_custom_call" | custom-call | tf_op jit(solution)/shard_map/hyena/pallas_call | solution.py:377
  67.3 0.0 copy-start
  67.4 1.7 %broadcast_multiply_fusion = f32[32,2048]{1,0:T(8,128)} fusion(f32[32,2048]{1,0:T(8,128)} %get-tuple-element.6), kind=kLoop, calls=%fused_computation.4 | loop fusion | flops 65536 | bytes 524288 | tf_op jit(solution)/shard_map/mul | solution.py:419
  69.1 0.0 copy-done.1
  69.1 0.0 copy-done.2
  69.1 0.0 copy-done.3
  69.1 0.0 copy-done.4
  69.1 0.0 copy-done
  69.1 2.5 %multiply_convert_fusion = (bf16[1,2048,128]{2,1,0:T(8,128)(2,1)}, bf16[1,2048,128]{2,1,0:T(8,128)(2,1)}) fusion(bf16[1,2048,128]{2,1,0:T(8,128)(2,1)S(1)} %copy-done, bf16[1,2048,128]{2,1,0:T(8,128)(2,1)} %bitcast.10, f32[2048]{0:T(1024)S(1)} %copy-done.4, bf16[1,2048,128]{2,1,0:T(8,128)(2,1)S(1)} %copy-done.2, bf16[1,2048,128]{2,1,0:T(8,128)(2,1)S(1)} %copy-done.1, ...), kind=kLoop, calls=%fused_computation.1 | loop fusion | flops 3670016 | bytes 3678208 | tf_op jit(solution)/shard_map/convert_element_type | solution.py:418
Async XLA Ops:
  0.6 68.5 %copy-start.1 = (bf16[1,2048,128]{2,1,0:T(8,128)(2,1)S(1)}, bf16[1,2048,128]{2,1,0:T(8,128)(2,1)}, u32[]{:S(2)}) copy-start(bf16[1,2048,128]{2,1,0:T(8,128)(2,1)} %param.6) | copy-start | bytes 1572868
  0.6 68.5 %copy-start.2 = (bf16[1,2048,128]{2,1,0:T(8,128)(2,1)S(1)}, bf16[1,2048,128]{2,1,0:T(8,128)(2,1)}, u32[]{:S(2)}) copy-start(bf16[1,2048,128]{2,1,0:T(8,128)(2,1)} %param.7) | copy-start | bytes 1572868
  0.7 68.4 %copy-start.3 = (bf16[1,2048,128]{2,1,0:T(8,128)(2,1)S(1)}, bf16[1,2048,128]{2,1,0:T(8,128)(2,1)}, u32[]{:S(2)}) copy-start(bf16[1,2048,128]{2,1,0:T(8,128)(2,1)} %param.9) | copy-start | bytes 1572868
  0.7 68.4 %copy-start.4 = (f32[2048]{0:T(1024)S(1)}, f32[2048]{0:T(1024)}, u32[]{:S(2)}) copy-start(f32[2048]{0:T(1024)} %param.11) | copy-start | bytes 24580
  67.3 1.8 %copy-start = (bf16[1,2048,128]{2,1,0:T(8,128)(2,1)S(1)}, bf16[1,2048,128]{2,1,0:T(8,128)(2,1)}, u32[]{:S(2)}) copy-start(bf16[1,2048,128]{2,1,0:T(8,128)(2,1)} %param.8) | copy-start | bytes 1572868

commit v3 on v2

--- a/solution.py
+++ b/solution.py
@@ -81,7 +81,7 @@
             for e in range(2):
                 blocks[pl.ds(pl.multiple_of((slot * 64 + m + e) * PITCH, 8), B), :] = out[:, e * B:(e + 1) * B]
 
-def fold(blocks, totals, step=16):
+def fold(blocks, totals, step=32):
     totals[...] = jnp.zeros(totals.shape, f32)
     rows = totals.shape[0]
     k = lax.broadcasted_iota(jnp.int32, (B, 2 * B), 0)
@@ -307,7 +307,7 @@
         c_z[7, n] = c_xy[n, :, 7]
 
     def multiply(first, last, base):
-        @pl.loop(first, last)
+        @pl.loop(first, last, unroll=True)
         def _(c):
             saved_t = srows[pl.ds(c, 256, stride=8), :].T.astype(bf16)
             product_blocks(saved_t, shifts, blocks, c, c - base)
@@ -322,12 +322,13 @@
 
     wait_31(s_all, xy_recv.at[1])
     unpack(s_all, srows)
-    multiply(0, 3, 0)
+    multiply(0, 2, 0)
     send_back(0)
-    multiply(3, 4, 0)
+    multiply(2, 4, 0)
     send_back(1)
     sum_up(0)
-    multiply(4, 8, 4)
+    multiply(4, 6, 4)
+    multiply(6, 8, 4)
     sum_up(4)
 
     for p in range(4):
@@ -364,6 +365,34 @@
     wait_31(g_all, xy_send.at[0])
     wait_31(s_all, xy_send.at[1])
     wait_31(c_own, xy_send.at[2])
+
+
+def finish_kernel(scale, c, go, pg, pre, val, skip, taps, gp, gv, out):
+    skip_t = skip[...].T
+    for n in range(8):
+        rows = pl.ds(n * B, B)
+        gated = (go[rows, :].astype(f32) * pg[rows, :].astype(f32)).astype(bf16).astype(f32)
+        summed = c[rows, :].astype(f32) + skip_t[:, n : n + 1] * gated
+        gp[rows, :] = (summed * val[rows, :].astype(f32)).astype(bf16)
+        gv[rows, :] = (summed * pre[rows, :].astype(f32)).astype(bf16)
+    out[...] = taps[...] * scale
+
+
+def finish(back, go, pg, pre, val, skip, taps, scale):
+    rows = pl.BlockSpec((1024, B), lambda n: (n, 0))
+    part = pl.BlockSpec((16, taps.shape[1]), lambda n: (n, 0))
+    return pl.pallas_call(
+        functools.partial(finish_kernel, scale),
+        grid=(2,),
+        out_shape=(
+            jax.ShapeDtypeStruct(go.shape, bf16),
+            jax.ShapeDtypeStruct(go.shape, bf16),
+            jax.ShapeDtypeStruct(taps.shape, f32),
+        ),
+        in_specs=[rows] * 5 + [pl.BlockSpec((8, B), lambda n: (n, 0)), part],
+        out_specs=(rows, rows, part),
+        name="finish",
+    )(back, go, pg, pre, val, skip, taps)
 
 
 def shards(grad_output, post_gate, pre_gate, value_branch, long_filter, skip_weight):
@@ -411,13 +440,11 @@
         ),
         name="hyena",
     )(grad_output[0], post_gate[0], pre_gate[0], value_branch[0], long_filter)
-    gated = (grad_output.astype(f32) * post_gate.astype(f32)).astype(bf16)
-    summed = back.reshape(1, channels, B).astype(f32) + skip_weight[None, :, None] * gated.astype(f32)
-    return (
-        (summed * value_branch.astype(f32)).astype(bf16),
-        (summed * pre_gate.astype(f32)).astype(bf16),
-        taps * (1.0 / math.sqrt(4 * length)),
+    gp, gv, taps = finish(
+        back.reshape(channels, B), grad_output[0], post_gate[0], pre_gate[0], value_branch[0],
+        skip_weight.reshape(16, B), taps, 1.0 / math.sqrt(4 * length),
     )
+    return gp[None], gv[None], taps
 
 
 def solution(mesh):

time: 71.8 us -> 69.5 us (0.968)
  other arithmetic: 4.23 us -> 0 us
  Pallas kernels: 66.7 us -> 68.8 us
    pallas_call x0 -> x1, Pallas kernels: none -> 2.96 us  [finish(): pl.pallas_call(functools.partial(finish_kernel, scale), grid=(2,), out_sh...]
    convert_element_type x1 -> x0, other arithmetic: 2.5 us -> none  [shards(): (summed * pre_gate.astype(f32)).astype(bf16)]
    mul x1 -> x0, other arithmetic: 1.73 us -> none  [shards(): taps * (1.0 / math.sqrt(4 * length))]
    pallas_call x1, Pallas kernels: 66.7 us -> 65.8 us  [shards(): pl.pallas_call(kernel, out_shape=(jax.ShapeDtypeStruct((8, 32, 8, B), bf1...]
where the time goes in v3:
time: 69.5 us; the launch traced here: 69.4 us
  Pallas kernels  68.8 us (99%)
    pallas_call x1, Pallas kernels, shards(): pl.pallas_call(kernel, out_shape=(jax.ShapeDtypeStruct((8, 32, 8, B), bf1...  65.8 us
    pallas_call x1, Pallas kernels, finish(): pl.pallas_call(functools.partial(finish_kernel, scale), grid=(2,), out_sh...  2.96 us

profile of v3, /device:TPU:1, one launch (start us, length us, event | category | flops | bytes accessed | tf_op | source)
XLA Modules:
  0.0 69.4 jit_solution(6944676163560685654)
XLA Ops:
  0.6 65.8 %hyena.1 = (bf16[8,32,8,128]{3,2,1,0:T(8,128)(2,1)}, f32[32,2048]{1,0:T(8,128)}) custom-call(bf16[2048,128]{1,0:T(8,128)(2,1)} %bitcast.8, bf16[2048,128]{1,0:T(8,128)(2,1)} %bitcast.10, bf16[2048,128]{1,0:T(8,128)(2,1)} %bitcast.12, bf16[2048,128]{1,0:T(8,128)(2,1)} %bitcast.14, f32[32,8192]{1,0:T(8,128)} %filt_hbm.1), custom_call_target="tpu_custom_call" | custom-call | tf_op jit(solution)/shard_map/hyena/pallas_call | solution.py:406
  66.4 3.0 %finish.1 = (bf16[2048,128]{1,0:T(8,128)(2,1)}, bf16[2048,128]{1,0:T(8,128)(2,1)}, f32[32,2048]{1,0:T(8,128)}) custom-call(bf16[2048,128]{1,0:T(8,128)(2,1)} %bitcast.16, bf16[2048,128]{1,0:T(8,128)(2,1)} %bitcast.9, bf16[2048,128]{1,0:T(8,128)(2,1)} %bitcast.11, bf16[2048,128]{1,0:T(8,128)(2,1)} %bitcast.13, bf16[2048,128]{1,0:T(8,128)(2,1)} %bitcast.15, ...), custom_call_target="tpu_custom_call" | custom-call | tf_op jit(solution)/shard_map/finish/pallas_call | solution.py:384

commit v4 on v3

--- a/solution.py
+++ b/solution.py
@@ -346,12 +346,14 @@
         t_sends[-1].start()
     t_all[0] = t_own[dp]
 
-    for send in c_sends:
-        send.wait_recv()
     for k in range(8):
+        if k < 7:
+            c_sends[k].wait_recv()
+            c_sends[7 + k].wait_recv()
+        there = z_peer(k, False)
         for n in range(2):
             for m in range(16):
-                back_ref[z_peer(k, False), 2 * m + n] = c_z[k, n, m]
+                back_ref[there, 2 * m + n] = c_z[k, n, m]
 
     for s in range(4):
         if s:

time: 69.5 us -> 69.5 us (level)
  no operation moved by 1% of the time
where the time goes in v4:
time: 69.5 us; the launch traced here: 69.4 us
  Pallas kernels  68.8 us (99%)
    pallas_call x1, Pallas kernels, shards(): pl.pallas_call(kernel, out_shape=(jax.ShapeDtypeStruct((8, 32, 8, B), bf1...  65.8 us
    pallas_call x1, Pallas kernels, finish(): pl.pallas_call(functools.partial(finish_kernel, scale), grid=(2,), out_sh...  2.96 us

profile of v4, /device:TPU:1, one launch (start us, length us, event | category | flops | bytes accessed | tf_op | source)
XLA Modules:
  0.0 69.4 jit_solution(1771002465196052837)
XLA Ops:
  0.6 65.8 %hyena.1 = (bf16[8,32,8,128]{3,2,1,0:T(8,128)(2,1)}, f32[32,2048]{1,0:T(8,128)}) custom-call(bf16[2048,128]{1,0:T(8,128)(2,1)} %bitcast.8, bf16[2048,128]{1,0:T(8,128)(2,1)} %bitcast.10, bf16[2048,128]{1,0:T(8,128)(2,1)} %bitcast.12, bf16[2048,128]{1,0:T(8,128)(2,1)} %bitcast.14, f32[32,8192]{1,0:T(8,128)} %filt_hbm.1), custom_call_target="tpu_custom_call" | custom-call | tf_op jit(solution)/shard_map/hyena/pallas_call | solution.py:408
  66.4 3.0 %finish.1 = (bf16[2048,128]{1,0:T(8,128)(2,1)}, bf16[2048,128]{1,0:T(8,128)(2,1)}, f32[32,2048]{1,0:T(8,128)}) custom-call(bf16[2048,128]{1,0:T(8,128)(2,1)} %bitcast.16, bf16[2048,128]{1,0:T(8,128)(2,1)} %bitcast.9, bf16[2048,128]{1,0:T(8,128)(2,1)} %bitcast.11, bf16[2048,128]{1,0:T(8,128)(2,1)} %bitcast.13, bf16[2048,128]{1,0:T(8,128)(2,1)} %bitcast.15, ...), custom_call_target="tpu_custom_call" | custom-call | tf_op jit(solution)/shard_map/finish/pallas_call | solution.py:386
